TPU v7x, 256 devices: a whole 4x4x8 slice. The times are simulated.
256 devices in a mesh: dp: 2 (over core), row: 32 (over z, x), col: 4 (over y).
Axes of the slice: x: 4, y: 4, z: 8, core: 2. Of those that a mesh axis runs over, the one named last changes fastest.
Arguments:
- layer_input: bfloat16 [1024, 8192], P('dp', 'col'), may hold values from -6 to 6
- out_grad: bfloat16 [1024, 8192], P('dp', 'col'), may hold values from -6 to 6
- w_gate: bfloat16 [8192, 14336], P('col', 'row'), may hold values from -0.0625 to 0.0625
- w_up: bfloat16 [8192, 14336], P('col', 'row'), may hold values from -0.0625 to 0.0625
- w_down: bfloat16 [14336, 8192], P('row', 'col'), may hold values from -0.046875 to 0.046875
Outputs:
- in_grad: bfloat16 [1024, 8192], P('dp', 'col')
- gate_grad: bfloat16 [8192, 14336], P(('col', 'dp'), 'row')
- up_grad: bfloat16 [8192, 14336], P(('col', 'dp'), 'row')
- down_grad: bfloat16 [14336, 8192], P('row', ('col', 'dp'))
All inputs are finite; a program needn't handle non-finite values.
Results may differ from a plain program's by a relative error of at most 0.0049.
Values may be sent and summed in bfloat16 or wider, within the bound.
A program may use at most 128 MiB of HBM per device.

v0:
```python
import jax
import jax.numpy as jnp
from jax import lax
from jax.sharding import PartitionSpec as P


def swiglu_back(gate_pre, up_pre, hid_grad):
    sigmoid = jax.nn.sigmoid(gate_pre)
    activation = gate_pre * sigmoid
    hidden = (activation * up_pre).astype(jnp.bfloat16)
    up_delta = (hid_grad * activation).astype(jnp.bfloat16)
    gate_delta = (hid_grad * up_pre * sigmoid * (1.0 + gate_pre * (1.0 - sigmoid))).astype(
        jnp.bfloat16
    )
    return (hidden, gate_delta, up_delta)


def contract_rows(left, right):
    return lax.dot_general(
        left, right, (((0,), (0,)), ((), ())), preferred_element_type=jnp.float32
    )


def contract_cols(left, right):
    return lax.dot_general(
        left, right, (((1,), (1,)), ((), ())), preferred_element_type=jnp.float32
    )


def body(layer_input, out_grad, w_gate, w_up, w_down):
    width_hid = w_gate.shape[1]
    gate_pre = jnp.dot(layer_input, w_gate, preferred_element_type=jnp.float32)
    up_pre = jnp.dot(layer_input, w_up, preferred_element_type=jnp.float32)
    hid_grad = contract_cols(out_grad, w_down)
    summed = lax.psum_scatter(
        jnp.concatenate((gate_pre, up_pre, hid_grad), axis=1),
        "col",
        scatter_dimension=0,
        tiled=True,
    )
    hidden, gate_delta, up_delta = swiglu_back(
        summed[:, :width_hid], summed[:, width_hid : 2 * width_hid], summed[:, 2 * width_hid :]
    )
    hidden_all, gate_all, up_all = (
        lax.all_gather(hidden, "col", axis=0, tiled=True),
        lax.all_gather(gate_delta, "col", axis=0, tiled=True),
        lax.all_gather(up_delta, "col", axis=0, tiled=True),
    )
    in_grad = lax.psum(contract_cols(gate_all, w_gate) + contract_cols(up_all, w_up), "row").astype(
        jnp.bfloat16
    )
    gate_term = contract_rows(layer_input, gate_all)
    up_term = contract_rows(layer_input, up_all)
    down_term = contract_rows(hidden_all, out_grad)
    gate_sum, up_sum, down_sum = (
        lax.psum_scatter(gate_term, "dp", scatter_dimension=0, tiled=True),
        lax.psum_scatter(up_term, "dp", scatter_dimension=0, tiled=True),
        lax.psum_scatter(down_term, "dp", scatter_dimension=1, tiled=True),
    )
    gate_grad = gate_sum.astype(jnp.bfloat16)
    up_grad = up_sum.astype(jnp.bfloat16)
    down_grad = down_sum.astype(jnp.bfloat16)
    return (in_grad, gate_grad, up_grad, down_grad)


def solution(mesh):
    placed = (P("dp", "col"), P("dp", "col"), P("col", "row"), P("col", "row"), P("row", "col"))
    return jax.shard_map(
        body,
        mesh=mesh,
        in_specs=placed,
        out_specs=(
            P("dp", "col"),
            P(("col", "dp"), "row"),
            P(("col", "dp"), "row"),
            P("row", ("col", "dp")),
        ),
        check_vma=False,
    )
```

profile of v0, /device:TPU:2, one launch (start us, length us, event | category | flops | bytes accessed | tf_op | source)
XLA Modules:
  0.0 300.4 jit_solution(7107233171609536599)
XLA Ops:
  7.2 0.0 copy-start
  7.2 0.0 reduce-scatter.5.cloned.1.call-start
  7.2 1.5 copy-done
  8.8 0.0 copy-start.2
  8.8 2.8 fusion.1
  11.5 0.0 copy-done.2
  11.6 0.0 copy-start.1
  11.6 0.0 copy-start.4
  11.6 1.1 fusion.2
  12.7 0.4 copy-done.1
  13.2 0.5 copy-done.4
  13.7 1.1 fusion.3
  14.8 1.8 pad_maximum_fusion
  16.7 0.0 reduce-scatter.5.cloned.1.call-update
  16.7 0.0 reduce-scatter.11.cloned.1.call-start
  16.7 40.7 %reduce-scatter.5.cloned.1.call-done = f32[128,1344]{0,1:T(8,128)} async-done(((f32[512,1344]{0,1:T(8,128)}), f32[128,1344]{0,1:T(8,128)}) %reduce-scatter.5.cloned.1.call-update) | async-done | bytes 688144 | tf_op jit(solution)/shard_map/reduce_scatter | solution.py:35
  57.4 1.3 multiply_convert_fusion
  58.7 13.0 %all_gather.11 = bf16[512,448]{0,1:T(8,128)(2,1)S(1)} all-gather(bf16[128,448]{0,1:T(8,128)(2,1)S(1)} %get-tuple-element.4), channel_id=1, replica_groups=mesh['dp'=2,'row'=32,'col'=4] {'col'}, dimensions={0}, use_global_device_ids=true | all-gather | bytes 573440 | tf_op jit(solution)/shard_map/all_gather | solution.py:45
  71.7 4.6 %fusion.5 = f32[448,2048]{1,0:T(8,128)} fusion(bf16[512,448]{0,1:T(8,128)(2,1)S(1)} %all_gather.11, bf16[512,2048]{1,0:T(8,128)(2,1)} %param.6), kind=kOutput, calls=%fused_computation.13 | convolution fusion | flops 939524096 | bytes 6225920 | tf_op jit(solution)/shard_map/dot_general | solution.py:19
  76.3 0.0 reduce-scatter.11.cloned.1.call-update
  76.4 0.0 reduce-scatter.9.cloned.1.call-start
  76.4 12.7 %all_gather.10 = bf16[512,448]{0,1:T(8,128)(2,1)S(1)} all-gather(bf16[128,448]{0,1:T(8,128)(2,1)S(1)} %get-tuple-element.6), channel_id=1, replica_groups=mesh['dp'=2,'row'=32,'col'=4] {'col'}, dimensions={0}, use_global_device_ids=true | all-gather | bytes 573440 | tf_op jit(solution)/shard_map/all_gather | solution.py:47
  89.1 3.1 %convolution_bitcast_fusion = f32[2048,448]{0,1:T(8,128)} fusion(bf16[512,448]{0,1:T(8,128)(2,1)S(1)} %all_gather.10, bf16[512,2048]{1,0:T(8,128)(2,1)S(1)} %copy-done), kind=kOutput, calls=%fused_computation.1 | convolution fusion | flops 939524096 | bytes 6225920 | tf_op jit(solution)/shard_map/dot_general | solution.py:19
  92.2 0.0 reduce-scatter.9.cloned.1.call-update
  92.2 0.0 reduce-scatter.7.cloned.1.call-start
  92.2 12.7 %all_gather.9 = bf16[512,448]{0,1:T(8,128)(2,1)S(1)} all-gather(bf16[128,448]{0,1:T(8,128)(2,1)S(1)} %get-tuple-element.5), channel_id=1, replica_groups=mesh['dp'=2,'row'=32,'col'=4] {'col'}, dimensions={0}, use_global_device_ids=true | all-gather | bytes 573440 | tf_op jit(solution)/shard_map/all_gather | solution.py:46
  104.9 2.9 convolution_bitcast_fusion.1
  107.8 0.0 reduce-scatter.7.cloned.1.call-update
  107.9 0.0 copy-start.3
  107.9 2.9 fusion.4
  110.8 0.0 copy-done.3
  110.8 3.3 %convolution_add_fusion = f32[512,2048]{1,0:T(8,128)} fusion(f32[512,2048]{1,0:T(8,128)S(1)} %fusion.4, bf16[512,448]{0,1:T(8,128)(2,1)S(1)} %all_gather.10, bf16[2048,448]{0,1:T(8,128)(2,1)S(1)} %copy-done.3), kind=kOutput, calls=%fused_computation | convolution fusion | flops 940572672 | bytes 10682368 | tf_op jit(solution)/shard_map/dot_general | solution.py:25
  114.1 172.0 %all-reduce.1 = bf16[512,2048]{1,0:T(8,128)(2,1)} all-reduce(f32[512,2048]{1,0:T(8,128)} %convolution_add_fusion), channel_id=1, replica_groups=mesh['dp'=2,'row'=32,'col'=4] {'row'}, use_global_device_ids=true, to_apply=%region_1.0 | all-reduce | flops 1048576 | bytes 6291456 | tf_op jit(solution)/shard_map/psum | solution.py:49
  286.1 0.0 reduce-scatter.11.cloned.1.call-done
  286.1 2.6 convert_element_type.27
  288.7 0.0 reduce-scatter.9.cloned.1.call-done
  288.7 2.6 convert_element_type.25
  291.3 0.0 reduce-scatter.7.cloned.1.call-done
  291.3 2.6 convert_element_type.24
Async XLA Ops:
  7.2 1.6 copy-start
  7.2 50.2 %reduce-scatter.5.cloned.1.call-start = ((), (), s32[]{:S(2)}) async-start(), calls=%async_computation.4 | async-start | bytes 3440640 | tf_op jit(solution)/shard_map/reduce_scatter | solution.py:35
  8.8 2.8 copy-start.2
  11.6 1.6 copy-start.1
  11.6 2.1 copy-start.4
  16.7 269.5 %reduce-scatter.11.cloned.1.call-start = ((), (), s32[]{:S(2)}) async-start(), calls=%async_computation.7 | async-start | bytes 5505024 | tf_op jit(solution)/shard_map/reduce_scatter | solution.py:58
  76.4 212.3 %reduce-scatter.9.cloned.1.call-start = ((), (), s32[]{:S(2)}) async-start(), calls=%async_computation.6 | async-start | bytes 5505024 | tf_op jit(solution)/shard_map/reduce_scatter | solution.py:57
  92.2 199.1 %reduce-scatter.7.cloned.1.call-start = ((), (), s32[]{:S(2)}) async-start(), calls=%async_computation.5 | async-start | bytes 5505024 | tf_op jit(solution)/shard_map/reduce_scatter | solution.py:56
  107.9 2.9 copy-start.3
Sparse Core Ops, SparseCore 0:
  16.8 40.5 reduce-scatter.4
  76.5 17.7 reduce-scatter.10
  96.9 18.1 reduce-scatter.8
  117.5 18.1 reduce-scatter.6
where the time goes:
time: 303 us; the launch traced here: 300 us
  blocking collectives  210 us (69%)
  waiting for transfers between devices  40.7 us (13%)
  matrix products  21.9 us (7%)
  between operations  13.8 us (5%)
  other arithmetic  10.8 us (4%)
    psum x1, blocking collectives, body(): lax.psum(contract_cols(gate_all, w_gate) + contract_cols(up_all, w_up), '...  172 us
    reduce_scatter x1, waiting for transfers between devices, body(): lax.psum_scatter(jnp.concatenate((gate_pre, up_pre, hid_grad), axis=1), '...  40.7 us
    all_gather x1, blocking collectives, body(): lax.all_gather(hidden, 'col', axis=0, tiled=True)  13 us
    all_gather x1, blocking collectives, body(): lax.all_gather(up_delta, 'col', axis=0, tiled=True)  12.7 us
    all_gather x1, blocking collectives, body(): lax.all_gather(gate_delta, 'col', axis=0, tiled=True)  12.7 us
    dot_general x3, matrix products, contract_rows(): lax.dot_general(left, right, (((0,), (0,)), ((), ())), preferred_element_...  10.6 us
    dot_general x3, matrix products, contract_cols(): lax.dot_general(left, right, (((1,), (1,)), ((), ())), preferred_element_...  7.37 us
  transfers between devices with their start and end apart: 4, of which 1 were waited for; matrix products, arithmetic and copies ran while one was open for 6% of the time, Pallas kernels for 0%

commit v1 on v0

v1 whole, which is shorter than its diff:
```python
import functools

import jax
import jax.numpy as jnp
from jax import lax
from jax.experimental import pallas as pl
from jax.experimental.pallas import tpu as pltpu
from jax.sharding import PartitionSpec as P

MESH = pl.DeviceIdType.MESH
BF16, F32 = jnp.bfloat16, jnp.float32
NX, NY, NZ = 4, 4, 8
TOK, WID, HID = 512, 2048, 448
CUT = 384
PACK = 3 * CUT + 256
HALF = WID // 2
ROUNDS = 2
SLAB = TOK // NY // ROUNDS
RTOK = TOK // ROUNDS
XCOL = WID // NX
ZROW = RTOK // NZ
ORDER = (
    ("f", 0), ("f", 1), ("s", 0), ("e", 0), ("e", 1), ("c", 0), ("c", 1), ("w", 0),
    ("x", 0), ("x", 1), ("w", 1), ("z", 0), ("z", 1), ("w", 2), ("a", 0), ("a", 1),
    ("o", 0), ("o", 1),
)


def dot(left, right, dims):
    return lax.dot_general(left, right, (dims, ((), ())), preferred_element_type=F32)


def pack(ref, first, second, third):
    dtype = ref.dtype
    for place, value in enumerate((first, second, third)):
        ref[:, place * CUT : (place + 1) * CUT] = value[:, :CUT].astype(dtype)
    tail = jnp.concatenate((first[:, CUT:], second[:, CUT:]), axis=1)
    ref[:, 3 * CUT : 3 * CUT + 128] = tail.astype(dtype)
    rest = jnp.concatenate((third[:, CUT:], jnp.zeros_like(third[:, CUT:])), axis=1)
    ref[:, 3 * CUT + 128 : PACK] = rest.astype(dtype)


def unpack(value):
    one, two = value[:, 3 * CUT : 3 * CUT + 128], value[:, 3 * CUT + 128 :]
    return (
        jnp.concatenate((value[:, :CUT], one[:, :64]), axis=1),
        jnp.concatenate((value[:, CUT : 2 * CUT], one[:, 64:]), axis=1),
        jnp.concatenate((value[:, 2 * CUT : 3 * CUT], two[:, :64]), axis=1),
    )


def kernel(
    x_hbm, g_hbm, wg_hbm, wu_hbm, wd_hbm, in_hbm, gate_hbm, up_hbm, down_hbm,
    xv, gv, wg, wu, wd, xs, gs, acc, ysend, yrecv, ag, agsib, delta, deltasib,
    xown, xsend, xrecv, zsend, zrecv, fin, gate_v, up_v, down_v,
    load_sem, out_sem, send_sem, recv_sem,
):
    dp, row, y = lax.axis_index("dp"), lax.axis_index("row"), lax.axis_index("col")
    z, x = row // NX, row % NX

    def at_y(k):
        return (dp, row, (y + k) % NY)

    def at_x(k):
        return (dp, z * NX + (x + k) % NX, y)

    def at_z(k):
        return (dp, ((z + k) % NZ) * NX + x, y)

    sibling = (1 - dp, row, y)

    barrier = pltpu.get_barrier_semaphore()
    partners = (
        [at_y(k) for k in range(1, NY)] + [at_x(k) for k in range(1, NX)] + [at_z(k) for k in range(1, NZ)] + [sibling]
    )
    for partner in partners:
        pl.semaphore_signal(barrier, inc=1, device_id=partner, device_id_type=MESH)

    loads = {}

    def load(name, src, dst):
        loads[name] = pltpu.make_async_copy(src, dst, load_sem.at[len(loads)])
        loads[name].start()

    def slab(p, k):
        return pl.ds(pl.multiple_of(((y + k) % NY) * (TOK // NY) + p * SLAB, SLAB), SLAB)

    def load_rows(name, src, dst, p):
        for k in range(NY):
            load((name, p, k), src.at[slab(p, k)], dst.at[pl.ds(p * RTOK + k * SLAB, SLAB)])

    load_rows("x", x_hbm, xv, 0)
    load("wg", wg_hbm, wg)
    load("wu", wu_hbm, wu)
    load_rows("g", g_hbm, gv, 0)
    load("wd", wd_hbm, wd)
    for p in range(1, ROUNDS):
        load_rows("x", x_hbm, xv, p)
        load_rows("g", g_hbm, gv, p)
    waited = set()

    def need(*names):
        for name in names:
            if name not in waited:
                waited.add(name)
                loads[name].wait()

    sends = {}

    def send(name, src, dst, device):
        n = len(sends)
        sends[name] = pltpu.make_async_remote_copy(
            src_ref=src, dst_ref=dst, send_sem=send_sem.at[n], recv_sem=recv_sem.at[n],
            device_id=device, device_id_type=MESH,
        )
        sends[name].start()

    def arrive(name):
        sends[name].wait_recv()

    outs = []

    def store(src, dst):
        outs.append(pltpu.make_async_copy(src, dst, out_sem.at[len(outs)]))
        outs[-1].start()

    def rows(p):
        return slice(p * RTOK, (p + 1) * RTOK)

    def forward(p):
        need(*[("x", p, k) for k in range(NY)], "wg")
        a = xv[rows(p)]
        gate = dot(a, wg[...], ((1,), (0,)))
        need("wu")
        up = dot(a, wu[...], ((1,), (0,)))
        need(*[("g", p, k) for k in range(NY)], "wd")
        hid = dot(gv[rows(p)], wd[...], ((1,), (1,)))
        pack(acc.at[p], gate[:SLAB], up[:SLAB], hid[:SLAB])
        pack(ysend.at[p], gate[SLAB:], up[SLAB:], hid[SLAB:])
        if p == 0:
            pl.semaphore_wait(barrier, len(partners))
        for k in (2, 1, 3):
            send(("yr", p, k), ysend.at[p, pl.ds((k - 1) * SLAB, SLAB)], yrecv.at[p, k - 1], at_y(k))

    def share(p):
        other = pl.ds(pl.multiple_of((1 - dp) * HALF, HALF), HALF)
        need(*[(name, q, k) for name in "xg" for q in range(ROUNDS) for k in range(NY)])
        send(("sx", 0), xv.at[:, other], xs, sibling)
        send(("sg", 0), gv.at[:, other], gs, sibling)

    def elementwise(p):
        for k in range(1, NY):
            arrive(("yr", p, k))
        gate, up, hid = unpack(
            acc[p] + yrecv[p, 0].astype(F32) + yrecv[p, 1].astype(F32) + yrecv[p, 2].astype(F32)
        )
        sig = jax.nn.sigmoid(gate)
        act = gate * sig
        pack(
            ag.at[p, pl.ds(0, SLAB)],
            hid * up * sig * (1.0 + gate * (1.0 - sig)), hid * act, act * up,
        )
        own = ag.at[p, pl.ds(0, SLAB)]
        for k in (2, 1, 3):
            send(("ya", p, k), own, ag.at[p, pl.ds((NY - k) * SLAB, SLAB)], at_y(k))

    def contract(p):
        for k in range(1, NY):
            arrive(("ya", p, k))
        send(("sd", p), ag.at[p], agsib.at[p], sibling)
        gd, ud, hd = unpack(ag[p])
        delta[0, rows(p)], delta[1, rows(p)], delta[2, rows(p)] = gd, ud, hd
        for k in (2, 1, 3, 0):
            block = pl.ds(pl.multiple_of(((x + k) % NX) * XCOL, XCOL), XCOL)
            part = dot(gd, wg[block, :], ((1,), (1,))) + dot(ud, wu[block, :], ((1,), (1,)))
            if k == 0:
                xown[p] = part
            else:
                xsend[p, k - 1] = part.astype(BF16)
                send(("xr", p, k), xsend.at[p, k - 1], xrecv.at[p, k - 1], at_x(k))

    def sum_x(p):
        for k in range(1, NX):
            arrive(("xr", p, k))
        xown[p] = xown[p] + xrecv[p, 0].astype(F32) + xrecv[p, 1].astype(F32) + xrecv[p, 2].astype(F32)
        for k in (4, 3, 5, 2, 6, 1, 7):
            part = pl.ds(pl.multiple_of(((z + k) % NZ) * ZROW, ZROW), ZROW)
            zsend[p, k - 1] = xown[p, part, :].astype(BF16)
            send(("zr", p, k), zsend.at[p, k - 1], zrecv.at[p, k - 1], at_z(k))

    def sum_z(p):
        for k in range(1, NZ):
            arrive(("zr", p, k))
        total = xown[p, pl.ds(pl.multiple_of(z * ZROW, ZROW), ZROW), :]
        for k in range(1, NZ):
            total = total + zrecv[p, k - 1].astype(F32)
        place = (
            pl.ds(pl.multiple_of(p * RTOK + z * ZROW, ZROW), ZROW),
            pl.ds(pl.multiple_of(x * XCOL, XCOL), XCOL),
        )
        fin[place] = total.astype(BF16)
        for k in (4, 3, 5, 2, 6, 1, 7):
            send(("za", p, k), fin.at[place], fin.at[place], at_z(k))

    def gather_x(p):
        for k in range(1, NZ):
            arrive(("za", p, k))
        place = fin.at[pl.ds(p * RTOK, RTOK), pl.ds(pl.multiple_of(x * XCOL, XCOL), XCOL)]
        for k in (2, 1, 3):
            send(("xa", p, k), place, place, at_x(k))

    def finish(p):
        for k in range(1, NX):
            arrive(("xa", p, k))
        for k in range(NY):
            store(fin.at[pl.ds(p * RTOK + k * SLAB, SLAB)], in_hbm.at[slab(p, k)])

    def weights(i):
        if i == 0:
            arrive(("sx", 0))
            arrive(("sg", 0))
            for p in range(ROUNDS):
                arrive(("sd", p))
                deltasib[0, rows(p)], deltasib[1, rows(p)], deltasib[2, rows(p)] = unpack(agsib[p])
        half = pl.ds(pl.multiple_of(dp * HALF, HALF), HALF)
        if i < 2:
            out, hbm = ((gate_v, gate_hbm), (up_v, up_hbm))[i]
            total = dot(xv[:, half], delta[i], ((0,), (0,))) + dot(xs[...], deltasib[i], ((0,), (0,)))
        else:
            out, hbm = down_v, down_hbm
            total = dot(delta[i], gv[:, half], ((0,), (0,))) + dot(deltasib[i], gs[...], ((0,), (0,)))
        out[...] = total.astype(BF16)
        store(out, hbm)

    tasks = {
        "f": forward, "s": share, "e": elementwise, "c": contract, "x": sum_x, "z": sum_z,
        "a": gather_x, "o": finish, "w": weights,
    }
    for name, i in ORDER:
        tasks[name](i)
    for copy in sends.values():
        copy.wait_send()
    for copy in outs:
        copy.wait()


def body(layer_input, out_grad, w_gate, w_up, w_down):
    n_sends = ROUNDS * (2 * (NY - 1) + 2 * (NX - 1) + 2 * (NZ - 1) + 1) + 2
    anywhere = pl.BlockSpec(memory_space=pl.ANY)
    return pl.pallas_call(
        kernel,
        out_shape=(
            jax.ShapeDtypeStruct((TOK, WID), BF16),
            jax.ShapeDtypeStruct((HALF, HID), BF16),
            jax.ShapeDtypeStruct((HALF, HID), BF16),
            jax.ShapeDtypeStruct((HID, HALF), BF16),
        ),
        in_specs=[anywhere] * 5,
        out_specs=[anywhere] * 4,
        scratch_shapes=[
            pltpu.VMEM((TOK, WID), BF16),
            pltpu.VMEM((TOK, WID), BF16),
            pltpu.VMEM((WID, HID), BF16),
            pltpu.VMEM((WID, HID), BF16),
            pltpu.VMEM((HID, WID), BF16),
            pltpu.VMEM((TOK, HALF), BF16),
            pltpu.VMEM((TOK, HALF), BF16),
            pltpu.VMEM((ROUNDS, SLAB, PACK), F32),
            pltpu.VMEM((ROUNDS, (NY - 1) * SLAB, PACK), BF16),
            pltpu.VMEM((ROUNDS, NY - 1, SLAB, PACK), BF16),
            pltpu.VMEM((ROUNDS, RTOK, PACK), BF16),
            pltpu.VMEM((ROUNDS, RTOK, PACK), BF16),
            pltpu.VMEM((3, TOK, HID), BF16),
            pltpu.VMEM((3, TOK, HID), BF16),
            pltpu.VMEM((ROUNDS, RTOK, XCOL), F32),
            pltpu.VMEM((ROUNDS, NX - 1, RTOK, XCOL), BF16),
            pltpu.VMEM((ROUNDS, NX - 1, RTOK, XCOL), BF16),
            pltpu.VMEM((ROUNDS, NZ - 1, ZROW, XCOL), BF16),
            pltpu.VMEM((ROUNDS, NZ - 1, ZROW, XCOL), BF16),
            pltpu.VMEM((TOK, WID), BF16),
            pltpu.VMEM((HALF, HID), BF16),
            pltpu.VMEM((HALF, HID), BF16),
            pltpu.VMEM((HID, HALF), BF16),
            pltpu.SemaphoreType.DMA((3 + 2 * NY * ROUNDS,)),
            pltpu.SemaphoreType.DMA((3 + NY * ROUNDS,)),
            pltpu.SemaphoreType.DMA((n_sends,)),
            pltpu.SemaphoreType.DMA((n_sends,)),
        ],
        compiler_params=pltpu.CompilerParams(
            collective_id=0, has_side_effects=True, vmem_limit_bytes=56 * 2**20
        ),
    )(layer_input, out_grad, w_gate, w_up, w_down)


def solution(mesh):
    placed = (P("dp", "col"), P("dp", "col"), P("col", "row"), P("col", "row"), P("row", "col"))
    return jax.shard_map(
        body,
        mesh=mesh,
        in_specs=placed,
        out_specs=(
            P("dp", "col"),
            P(("col", "dp"), "row"),
            P(("col", "dp"), "row"),
            P("row", ("col", "dp")),
        ),
        check_vma=False,
    )
```

time: 303 us -> 116 us (0.38)
  blocking collectives: 210 us -> 0 us
  Pallas kernels: 0 us -> 102 us
  waiting for transfers between devices: 40.7 us -> 0 us
  matrix products: 21.9 us -> 0 us
  between operations: 13.8 us -> 0.66 us
  local copies, waits for them, and re-layouts: 2.52 us -> 13.7 us
  other arithmetic: 10.8 us -> 0 us
    psum x1 -> x0, blocking collectives: 172 us -> none  [body(): lax.psum(contract_cols(gate_all, w_gate) + contract_cols(up_all, w_up), '...]
    pallas_call x0 -> x1, Pallas kernels: none -> 102 us  [body(): pl.pallas_call(kernel, out_shape=(jax.ShapeDtypeStruct((TOK, WID), BF16),...]
    reduce_scatter x4 -> x0, waiting for transfers between devices: 40.7 us -> none  [the longest x1 40.7 us: body(): lax.psum_scatter(jnp.concatenate((gate_pre, up_pre, hid_grad), axis=1), '...]
    all_gather x3 -> x0, blocking collectives: 38.4 us -> none  [the longest x1 13 us: body(): lax.all_gather(hidden, 'col', axis=0, tiled=True)]
    dot_general x8 -> x0, matrix products: 21.9 us -> none  [the longest x3 10.6 us: contract_rows(): lax.dot_general(left, right, (((0,), (0,)), ((), ())), preferred_element_...]
    convert_element_type x4 -> x0, other arithmetic: 8.99 us -> none  [the longest x1 2.56 us: body(): gate_grad = gate_sum.astype(jnp.bfloat16)]
    unnamed x10, local copies, waits for them, and re-layouts: 2.52 us -> 9.1 us
    pallas_call x0 -> x2, local copies, waits for them, and re-layouts: none -> 4.58 us  [body(): pl.pallas_call(kernel, out_shape=(jax.ShapeDtypeStruct((TOK, WID), BF16),...]
  transfers between devices with their start and end apart: 4 -> 0, of which waited for: 1 -> 0; matrix products, arithmetic and copies ran while one was open for 6% -> 0% of each run, Pallas kernels for 0% -> 0%
where the time goes in v1:
time: 116 us
  Pallas kernels  102 us (88%)
  local copies, waits for them, and re-layouts  13.7 us (12%)
    pallas_call x1, Pallas kernels, body(): pl.pallas_call(kernel, out_shape=(jax.ShapeDtypeStruct((TOK, WID), BF16),...  102 us
    unnamed x10, local copies, waits for them, and re-layouts  9.1 us
    pallas_call x2, local copies, waits for them, and re-layouts, body(): pl.pallas_call(kernel, out_shape=(jax.ShapeDtypeStruct((TOK, WID), BF16),...  4.58 us

profile of v1, /device:TPU:2, one launch (start us, length us, event | category | flops | bytes accessed | tf_op | source)
XLA Modules:
  0.0 116.0 jit_solution(522088318886462552)
XLA Ops:
  0.6 0.0 copy-start.1
  0.6 3.9 %copy.9.wg_hbm = bf16[2048,448]{1,0:T(8,128)(2,1)} copy(bf16[2048,448]{0,1:T(8,128)(2,1)} %param.7) | data formatting | bytes 3670016 | tf_op args[2]
  4.6 0.0 copy-done.1
  4.6 2.4 %copy.10.wu_hbm = bf16[2048,448]{1,0:T(8,128)(2,1)} copy(bf16[2048,448]{0,1:T(8,128)(2,1)S(1)} %copy-done.1) | data formatting | bytes 3670016 | tf_op args[3]
  7.0 101.7 %shard_map.84 = (bf16[512,2048]{1,0:T(8,128)(2,1)}, bf16[1024,448]{1,0:T(8,128)(2,1)}, bf16[1024,448]{1,0:T(8,128)(2,1)}, bf16[448,1024]{1,0:T(8,128)(2,1)}) custom-call(bf16[512,2048]{1,0:T(8,128)(2,1)} %x_hbm.1, bf16[512,2048]{1,0:T(8,128)(2,1)} %g_hbm.1, bf16[2048,448]{1,0:T(8,128)(2,1)} %copy.9.wg_hbm, bf16[2048,448]{1,0:T(8,128)(2,1)} %copy.10.wu_hbm, ...), custom_call_target="tpu_custom_call" | custom-call | tf_op jit(solution)/shard_map/pallas_call | solution.py:250
  108.7 0.0 copy-start
  108.7 2.4 %copy.11 = bf16[1024,448]{0,1:T(8,128)(2,1)} copy(bf16[1024,448]{1,0:T(8,128)(2,1)} %get-tuple-element.5) | data formatting | bytes 1835008 | tf_op jit(solution)/shard_map/pallas_call | solution.py:250
  111.1 2.2 %copy.12 = bf16[1024,448]{0,1:T(8,128)(2,1)} copy(bf16[1024,448]{1,0:T(8,128)(2,1)} %get-tuple-element.6) | data formatting | bytes 1835008 | tf_op jit(solution)/shard_map/pallas_call | solution.py:250
  113.3 0.0 copy-done
  113.3 0.0 copy-start.2
  113.3 1.3 %copy.15 = bf16[512,2048]{1,0:T(8,128)(2,1)} copy(bf16[512,2048]{1,0:T(8,128)(2,1)S(1)} %copy-done) | data formatting | bytes 4194304
  114.6 0.5 copy-done.2
  115.1 0.9 copy.16
Async XLA Ops:
  0.6 4.0 %copy-start.1 = (bf16[2048,448]{0,1:T(8,128)(2,1)S(1)}, bf16[2048,448]{0,1:T(8,128)(2,1)}, u32[]{:S(2)}) copy-start(bf16[2048,448]{0,1:T(8,128)(2,1)} %param.8) | copy-start | bytes 5505028
  108.7 4.6 %copy-start = (bf16[512,2048]{1,0:T(8,128)(2,1)S(1)}, bf16[512,2048]{1,0:T(8,128)(2,1)}, u32[]{:S(2)}) copy-start(bf16[512,2048]{1,0:T(8,128)(2,1)} %get-tuple-element.12) | copy-start | bytes 6291460
  113.3 1.8 %copy-start.2 = (bf16[448,1024]{1,0:T(8,128)(2,1)S(1)}, bf16[448,1024]{1,0:T(8,128)(2,1)}, u32[]{:S(2)}) copy-start(bf16[448,1024]{1,0:T(8,128)(2,1)} %get-tuple-element.15) | copy-start | bytes 2752516

commit v2 on v1

--- a/solution.py
+++ b/solution.py
@@ -14,15 +14,20 @@
 CUT = 384
 PACK = 3 * CUT + 256
 HALF = WID // 2
-ROUNDS = 2
+ROUNDS = 4
 SLAB = TOK // NY // ROUNDS
 RTOK = TOK // ROUNDS
 XCOL = WID // NX
 ZROW = RTOK // NZ
 ORDER = (
-    ("f", 0), ("f", 1), ("s", 0), ("e", 0), ("e", 1), ("c", 0), ("c", 1), ("w", 0),
-    ("x", 0), ("x", 1), ("w", 1), ("z", 0), ("z", 1), ("w", 2), ("a", 0), ("a", 1),
-    ("o", 0), ("o", 1),
+    ("F", 0), ("F", 1), ("H", 0), ("Y", 0, 0), ("Y", 0, 1), ("Y", 1, 0), ("Y", 1, 1), ("E", 0), ("F", 2),
+    ("E", 1), ("F", 3), ("G", 0, 0), ("G", 0, 1), ("Y", 2, 0), ("Y", 2, 1), ("G", 1, 0), ("G", 1, 1),
+    ("Y", 3, 0), ("Y", 3, 1), ("C", 0), ("E", 2), ("C", 1), ("E", 3), ("X", 0, 0), ("X", 0, 1), ("G", 2, 0),
+    ("G", 2, 1), ("X", 1, 0), ("X", 1, 1), ("G", 3, 0), ("G", 3, 1), ("C", 2), ("S", 0), ("C", 3), ("S", 1),
+    ("W", 0), ("X", 2, 0), ("X", 2, 1), ("W", 1), ("W", 2), ("X", 3, 0), ("X", 3, 1), ("W", 3), ("T", 0),
+    ("W", 4), ("W", 5), ("S", 2), ("T", 1), ("S", 3), ("A", 0), ("T", 2), ("B", 0, 0), ("B", 0, 1), ("A", 1),
+    ("T", 3), ("O", 0), ("A", 2), ("B", 1, 0), ("B", 1, 1), ("A", 3), ("B", 2, 0), ("B", 2, 1), ("O", 1),
+    ("B", 3, 0), ("B", 3, 1), ("O", 2), ("O", 3),
 )
 
 
@@ -51,8 +56,8 @@
 
 def kernel(
     x_hbm, g_hbm, wg_hbm, wu_hbm, wd_hbm, in_hbm, gate_hbm, up_hbm, down_hbm,
-    xv, gv, wg, wu, wd, xs, gs, acc, ysend, yrecv, ag, agsib, delta, deltasib,
-    xown, xsend, xrecv, zsend, zrecv, fin, gate_v, up_v, down_v,
+    xv, gv, wg, wu, wd, xs, gs, yown, yacc, ysend, yone, ytwo, ag, agsib, delta, deltasib,
+    xown, xacc, xsend, xone, xtwo, zsend, zrecv, fin, gate_v, up_v, down_v,
     load_sem, out_sem, send_sem, recv_sem,
 ):
     dp, row, y = lax.axis_index("dp"), lax.axis_index("row"), lax.axis_index("col")
@@ -71,7 +76,7 @@
 
     barrier = pltpu.get_barrier_semaphore()
     partners = (
-        [at_y(k) for k in range(1, NY)] + [at_x(k) for k in range(1, NX)] + [at_z(k) for k in range(1, NZ)] + [sibling]
+        [at_y(1), at_y(3), at_x(1), at_x(3)] + [at_z(k) for k in range(1, NZ)] + [sibling]
     )
     for partner in partners:
         pl.semaphore_signal(barrier, inc=1, device_id=partner, device_id_type=MESH)
@@ -127,20 +132,56 @@
     def rows(p):
         return slice(p * RTOK, (p + 1) * RTOK)
 
+    def ring_start(tag, p, at, parts, one, two):
+        h = parts[1].shape[0] // 2
+        lo, hi = pl.ds(0, h), pl.ds(h, h)
+        send((tag + "1", p, 0), parts[2].at[lo], one.at[p, 0], at(1))
+        send((tag + "1", p, 1), parts[2].at[hi], one.at[p, 1], at(3))
+        send((tag + "2", p, 0), parts[1].at[hi], two.at[p, 0, hi], at(1))
+        send((tag + "2", p, 1), parts[3].at[lo], two.at[p, 1, lo], at(3))
+
+    def ring_add(tag, p, way, at, part, acc, one, two):
+        arrive((tag + "1", p, way))
+        h = part.shape[0] // 2
+        mine = pl.ds(way * h, h)
+        part[mine, :] = (acc[p, way] + one[p, way].astype(F32)).astype(BF16)
+        send((tag + "3", p, way), part.at[mine], two.at[p, way, mine], at(1 + 2 * way))
+
+    def ring_sum(tag, p, own, two):
+        for way in range(2):
+            arrive((tag + "2", p, way))
+            arrive((tag + "3", p, way))
+        return own + two[p, 0].astype(F32) + two[p, 1].astype(F32)
+
+    def yparts(p):
+        return {k: ysend.at[p, k - 1] for k in (1, 2, 3)}
+
+    def xparts(p):
+        return {k: xsend.at[p, k - 1] for k in (1, 2, 3)}
+
     def forward(p):
         need(*[("x", p, k) for k in range(NY)], "wg")
         a = xv[rows(p)]
-        gate = dot(a, wg[...], ((1,), (0,)))
+        gate = dot(a, wg[...], ((1,), (1,)))
         need("wu")
-        up = dot(a, wu[...], ((1,), (0,)))
+        up = dot(a, wu[...], ((1,), (1,)))
         need(*[("g", p, k) for k in range(NY)], "wd")
         hid = dot(gv[rows(p)], wd[...], ((1,), (1,)))
-        pack(acc.at[p], gate[:SLAB], up[:SLAB], hid[:SLAB])
-        pack(ysend.at[p], gate[SLAB:], up[SLAB:], hid[SLAB:])
+
+        def put(ref, start, stop):
+            pack(ref, gate[start:stop], up[start:stop], hid[start:stop])
+
+        for k in (2, 1, 3):
+            put(ysend.at[p, k - 1], k * SLAB, (k + 1) * SLAB)
         if p == 0:
             pl.semaphore_wait(barrier, len(partners))
-        for k in (2, 1, 3):
-            send(("yr", p, k), ysend.at[p, pl.ds((k - 1) * SLAB, SLAB)], yrecv.at[p, k - 1], at_y(k))
+        ring_start("y", p, at_y, yparts(p), yone, ytwo)
+        put(yacc.at[p, 0], SLAB, SLAB + SLAB // 2)
+        put(yacc.at[p, 1], 3 * SLAB + SLAB // 2, 4 * SLAB)
+        put(yown.at[p], 0, SLAB)
+
+    def add_y(p, way):
+        ring_add("y", p, way, at_y, yparts(p)[1 + 2 * way], yacc, yone, ytwo)
 
     def share(p):
         other = pl.ds(pl.multiple_of((1 - dp) * HALF, HALF), HALF)
@@ -149,11 +190,7 @@
         send(("sg", 0), gv.at[:, other], gs, sibling)
 
     def elementwise(p):
-        for k in range(1, NY):
-            arrive(("yr", p, k))
-        gate, up, hid = unpack(
-            acc[p] + yrecv[p, 0].astype(F32) + yrecv[p, 1].astype(F32) + yrecv[p, 2].astype(F32)
-        )
+        gate, up, hid = unpack(ring_sum("y", p, yown[p], ytwo))
         sig = jax.nn.sigmoid(gate)
         act = gate * sig
         pack(
@@ -161,28 +198,40 @@
             hid * up * sig * (1.0 + gate * (1.0 - sig)), hid * act, act * up,
         )
         own = ag.at[p, pl.ds(0, SLAB)]
-        for k in (2, 1, 3):
-            send(("ya", p, k), own, ag.at[p, pl.ds((NY - k) * SLAB, SLAB)], at_y(k))
+        send(("g1", p, 0), own, ag.at[p, pl.ds(3 * SLAB, SLAB)], at_y(1))
+        send(("g1", p, 1), own, ag.at[p, pl.ds(SLAB, SLAB)], at_y(3))
+
+    def pass_y(p, way):
+        arrive(("g1", p, way))
+        h = SLAB // 2
+        src = ag.at[p, pl.ds((3 - 2 * way) * SLAB + way * h, h)]
+        send(("g2", p, way), src, ag.at[p, pl.ds(2 * SLAB + way * h, h)], at_y(1 + 2 * way))
 
     def contract(p):
-        for k in range(1, NY):
-            arrive(("ya", p, k))
+        for way in range(2):
+            arrive(("g2", p, way))
         send(("sd", p), ag.at[p], agsib.at[p], sibling)
         gd, ud, hd = unpack(ag[p])
         delta[0, rows(p)], delta[1, rows(p)], delta[2, rows(p)] = gd, ud, hd
+        h = RTOK // 2
         for k in (2, 1, 3, 0):
             block = pl.ds(pl.multiple_of(((x + k) % NX) * XCOL, XCOL), XCOL)
-            part = dot(gd, wg[block, :], ((1,), (1,))) + dot(ud, wu[block, :], ((1,), (1,)))
+            part = dot(gd, wg[:, block], ((1,), (0,))) + dot(ud, wu[:, block], ((1,), (0,)))
             if k == 0:
                 xown[p] = part
             else:
                 xsend[p, k - 1] = part.astype(BF16)
-                send(("xr", p, k), xsend.at[p, k - 1], xrecv.at[p, k - 1], at_x(k))
+            if k == 1:
+                xacc[p, 0] = part[:h]
+            if k == 3:
+                xacc[p, 1] = part[h:]
+                ring_start("x", p, at_x, xparts(p), xone, xtwo)
+
+    def add_x(p, way):
+        ring_add("x", p, way, at_x, xparts(p)[1 + 2 * way], xacc, xone, xtwo)
 
     def sum_x(p):
-        for k in range(1, NX):
-            arrive(("xr", p, k))
-        xown[p] = xown[p] + xrecv[p, 0].astype(F32) + xrecv[p, 1].astype(F32) + xrecv[p, 2].astype(F32)
+        xown[p] = ring_sum("x", p, xown[p], xtwo)
         for k in (4, 3, 5, 2, 6, 1, 7):
             part = pl.ds(pl.multiple_of(((z + k) % NZ) * ZROW, ZROW), ZROW)
             zsend[p, k - 1] = xown[p, part, :].astype(BF16)
@@ -202,16 +251,28 @@
         for k in (4, 3, 5, 2, 6, 1, 7):
             send(("za", p, k), fin.at[place], fin.at[place], at_z(k))
 
+    def xplace(p, k, start, size):
+        return fin.at[
+            pl.ds(p * RTOK + start, size),
+            pl.ds(pl.multiple_of(((x + k) % NX) * XCOL, XCOL), XCOL),
+        ]
+
     def gather_x(p):
         for k in range(1, NZ):
             arrive(("za", p, k))
-        place = fin.at[pl.ds(p * RTOK, RTOK), pl.ds(pl.multiple_of(x * XCOL, XCOL), XCOL)]
-        for k in (2, 1, 3):
-            send(("xa", p, k), place, place, at_x(k))
+        place = xplace(p, 0, 0, RTOK)
+        for way in range(2):
+            send(("b1", p, way), place, place, at_x(1 + 2 * way))
+
+    def pass_x(p, way):
+        arrive(("b1", p, way))
+        h = RTOK // 2
+        place = xplace(p, 3 - 2 * way, way * h, h)
+        send(("b2", p, way), place, place, at_x(1 + 2 * way))
 
     def finish(p):
-        for k in range(1, NX):
-            arrive(("xa", p, k))
+        for way in range(2):
+            arrive(("b2", p, way))
         for k in range(NY):
             store(fin.at[pl.ds(p * RTOK + k * SLAB, SLAB)], in_hbm.at[slab(p, k)])
 
@@ -222,22 +283,23 @@
             for p in range(ROUNDS):
                 arrive(("sd", p))
                 deltasib[0, rows(p)], deltasib[1, rows(p)], deltasib[2, rows(p)] = unpack(agsib[p])
-        half = pl.ds(pl.multiple_of(dp * HALF, HALF), HALF)
-        if i < 2:
-            out, hbm = ((gate_v, gate_hbm), (up_v, up_hbm))[i]
-            total = dot(xv[:, half], delta[i], ((0,), (0,))) + dot(xs[...], deltasib[i], ((0,), (0,)))
-        else:
-            out, hbm = down_v, down_hbm
-            total = dot(delta[i], gv[:, half], ((0,), (0,))) + dot(deltasib[i], gs[...], ((0,), (0,)))
-        out[...] = total.astype(BF16)
-        store(out, hbm)
+        i, j = i // 2, i % 2
+        out, hbm = ((gate_v, gate_hbm), (up_v, up_hbm), (down_v, down_hbm))[i]
+        own, sib = (gv, gs) if i == 2 else (xv, xs)
+        w = HALF // 2
+        half = pl.ds(pl.multiple_of(dp * HALF + j * w, w), w)
+        part = pl.ds(j * w, w)
+        total = dot(delta[i], own[:, half], ((0,), (0,))) + dot(deltasib[i], sib[:, part], ((0,), (0,)))
+        out[:, part] = total.astype(BF16)
+        if j == 1:
+            store(out, hbm)
 
     tasks = {
-        "f": forward, "s": share, "e": elementwise, "c": contract, "x": sum_x, "z": sum_z,
-        "a": gather_x, "o": finish, "w": weights,
+        "F": forward, "H": share, "Y": add_y, "E": elementwise, "G": pass_y, "C": contract,
+        "X": add_x, "S": sum_x, "T": sum_z, "A": gather_x, "B": pass_x, "O": finish, "W": weights,
     }
-    for name, i in ORDER:
-        tasks[name](i)
+    for name, *args in ORDER:
+        tasks[name](*args)
     for copy in sends.values():
         copy.wait_send()
     for copy in outs:
@@ -245,14 +307,14 @@
 
 
 def body(layer_input, out_grad, w_gate, w_up, w_down):
-    n_sends = ROUNDS * (2 * (NY - 1) + 2 * (NX - 1) + 2 * (NZ - 1) + 1) + 2
+    n_sends = ROUNDS * (2 * (6 + 4) + 2 * (NZ - 1) + 1) + 2
     anywhere = pl.BlockSpec(memory_space=pl.ANY)
-    return pl.pallas_call(
+    in_grad, gate_grad, up_grad, down_grad = pl.pallas_call(
         kernel,
         out_shape=(
             jax.ShapeDtypeStruct((TOK, WID), BF16),
-            jax.ShapeDtypeStruct((HALF, HID), BF16),
-            jax.ShapeDtypeStruct((HALF, HID), BF16),
+            jax.ShapeDtypeStruct((HID, HALF), BF16),
+            jax.ShapeDtypeStruct((HID, HALF), BF16),
             jax.ShapeDtypeStruct((HID, HALF), BF16),
         ),
         in_specs=[anywhere] * 5,
@@ -260,26 +322,30 @@
         scratch_shapes=[
             pltpu.VMEM((TOK, WID), BF16),
             pltpu.VMEM((TOK, WID), BF16),
-            pltpu.VMEM((WID, HID), BF16),
-            pltpu.VMEM((WID, HID), BF16),
+            pltpu.VMEM((HID, WID), BF16),
+            pltpu.VMEM((HID, WID), BF16),
             pltpu.VMEM((HID, WID), BF16),
             pltpu.VMEM((TOK, HALF), BF16),
             pltpu.VMEM((TOK, HALF), BF16),
             pltpu.VMEM((ROUNDS, SLAB, PACK), F32),
-            pltpu.VMEM((ROUNDS, (NY - 1) * SLAB, PACK), BF16),
+            pltpu.VMEM((ROUNDS, 2, SLAB // 2, PACK), F32),
             pltpu.VMEM((ROUNDS, NY - 1, SLAB, PACK), BF16),
+            pltpu.VMEM((ROUNDS, 2, SLAB // 2, PACK), BF16),
+            pltpu.VMEM((ROUNDS, 2, SLAB, PACK), BF16),
             pltpu.VMEM((ROUNDS, RTOK, PACK), BF16),
             pltpu.VMEM((ROUNDS, RTOK, PACK), BF16),
             pltpu.VMEM((3, TOK, HID), BF16),
             pltpu.VMEM((3, TOK, HID), BF16),
             pltpu.VMEM((ROUNDS, RTOK, XCOL), F32),
+            pltpu.VMEM((ROUNDS, 2, RTOK // 2, XCOL), F32),
             pltpu.VMEM((ROUNDS, NX - 1, RTOK, XCOL), BF16),
-            pltpu.VMEM((ROUNDS, NX - 1, RTOK, XCOL), BF16),
+            pltpu.VMEM((ROUNDS, 2, RTOK // 2, XCOL), BF16),
+            pltpu.VMEM((ROUNDS, 2, RTOK, XCOL), BF16),
             pltpu.VMEM((ROUNDS, NZ - 1, ZROW, XCOL), BF16),
             pltpu.VMEM((ROUNDS, NZ - 1, ZROW, XCOL), BF16),
             pltpu.VMEM((TOK, WID), BF16),
-            pltpu.VMEM((HALF, HID), BF16),
-            pltpu.VMEM((HALF, HID), BF16),
+            pltpu.VMEM((HID, HALF), BF16),
+            pltpu.VMEM((HID, HALF), BF16),
             pltpu.VMEM((HID, HALF), BF16),
             pltpu.SemaphoreType.DMA((3 + 2 * NY * ROUNDS,)),
             pltpu.SemaphoreType.DMA((3 + NY * ROUNDS,)),
@@ -289,7 +355,8 @@
         compiler_params=pltpu.CompilerParams(
             collective_id=0, has_side_effects=True, vmem_limit_bytes=56 * 2**20
         ),
-    )(layer_input, out_grad, w_gate, w_up, w_down)
+    )(layer_input, out_grad, w_gate.T, w_up.T, w_down)
+    return in_grad, gate_grad.T, up_grad.T, down_grad
 
 
 def solution(mesh):

time: 116 us -> 87.2 us (0.75)
  Pallas kernels: 102 us -> 80.4 us
  local copies, waits for them, and re-layouts: 13.7 us -> 6.07 us
    pallas_call x1, Pallas kernels: 102 us -> 80.4 us  [body(): pl.pallas_call(kernel, out_shape=(jax.ShapeDtypeStruct((TOK, WID), BF16),...]
    pallas_call x2 -> x0, local copies, waits for them, and re-layouts: 4.58 us -> none  [body(): pl.pallas_call(kernel, out_shape=(jax.ShapeDtypeStruct((TOK, WID), BF16),...]
    unnamed x10, local copies, waits for them, and re-layouts: 9.1 us -> 6.07 us
where the time goes in v2:
time: 87.2 us; the launch traced here: 87.1 us
  Pallas kernels  80.4 us (92%)
  local copies, waits for them, and re-layouts  6.07 us (7%)
    pallas_call x1, Pallas kernels, body(): pl.pallas_call(kernel, out_shape=(jax.ShapeDtypeStruct((TOK, WID), BF16),...  80.4 us
    unnamed x10, local copies, waits for them, and re-layouts  6.07 us

profile of v2, /device:TPU:2, one launch (start us, length us, event | category | flops | bytes accessed | tf_op | source)
XLA Modules:
  0.0 87.1 jit_solution(13134012694221611984)
XLA Ops:
  0.6 80.4 %shard_map.84 = (bf16[512,2048]{1,0:T(8,128)(2,1)}, bf16[448,1024]{1,0:T(8,128)(2,1)}, bf16[448,1024]{1,0:T(8,128)(2,1)}, bf16[448,1024]{1,0:T(8,128)(2,1)}) custom-call(bf16[512,2048]{1,0:T(8,128)(2,1)} %x_hbm.1, bf16[512,2048]{1,0:T(8,128)(2,1)} %g_hbm.1, bf16[448,2048]{1,0:T(8,128)(2,1)} %bitcast.4, bf16[448,2048]{1,0:T(8,128)(2,1)} %bitcast.5, ...), custom_call_target="tpu_custom_call" | custom-call | tf_op jit(solution)/shard_map/pallas_call | solution.py:312
  81.0 0.0 copy-start.2
  81.0 0.0 copy-start.1
  81.0 3.3 %copy.13 = bf16[512,2048]{1,0:T(8,128)(2,1)} copy(bf16[512,2048]{1,0:T(8,128)(2,1)} %get-tuple-element.16) | data formatting | bytes 4194304
  84.3 0.0 copy-done.2
  84.3 0.0 copy-start
  84.3 0.9 %copy.14 = bf16[1024,448]{0,1:T(8,128)(2,1)} copy(bf16[1024,448]{0,1:T(8,128)(2,1)S(1)} %bitcast.7) | data formatting | bytes 1835008
  85.3 0.0 copy-done.1
  85.3 0.9 %copy.15 = bf16[1024,448]{0,1:T(8,128)(2,1)} copy(bf16[1024,448]{0,1:T(8,128)(2,1)S(1)} %bitcast.6) | data formatting | bytes 1835008
  86.2 0.0 copy-done
  86.2 0.9 %copy.16 = bf16[448,1024]{1,0:T(8,128)(2,1)} copy(bf16[448,1024]{1,0:T(8,128)(2,1)S(1)} %copy-done) | data formatting | bytes 1835008
Async XLA Ops:
  81.0 3.3 %copy-start.2 = (bf16[448,1024]{1,0:T(8,128)(2,1)S(1)}, bf16[448,1024]{1,0:T(8,128)(2,1)}, u32[]{:S(2)}) copy-start(bf16[448,1024]{1,0:T(8,128)(2,1)} %get-tuple-element.9) | copy-start | bytes 2752516
  81.0 4.2 %copy-start.1 = (bf16[448,1024]{1,0:T(8,128)(2,1)S(1)}, bf16[448,1024]{1,0:T(8,128)(2,1)}, u32[]{:S(2)}) copy-start(bf16[448,1024]{1,0:T(8,128)(2,1)} %get-tuple-element.10) | copy-start | bytes 2752516
  84.3 1.9 %copy-start = (bf16[448,1024]{1,0:T(8,128)(2,1)S(1)}, bf16[448,1024]{1,0:T(8,128)(2,1)}, u32[]{:S(2)}) copy-start(bf16[448,1024]{1,0:T(8,128)(2,1)} %get-tuple-element.19) | copy-start | bytes 2752516

commit v3 on v0

v3 whole, which is shorter than its diff:
```python
import jax
import jax.numpy as jnp
from jax import lax
from jax.experimental import pallas as pl
from jax.experimental.pallas import tpu as pltpu
from jax.sharding import PartitionSpec as P

MESH = pl.DeviceIdType.MESH
BF16, F32 = jnp.bfloat16, jnp.float32
NX, NY, NZ = 4, 4, 8
TOK, WID, HID = 512, 2048, 448
CUT = 384
BOTH = 2 * HID
PACK = BOTH + 512
HALF = WID // 2
OWN = TOK // NY
ROUNDS = 8
BATCHES = ((0,), (1, 2), (3, 4), (5, 6, 7))
SLAB = OWN // ROUNDS
RTOK = TOK // ROUNDS
XCOL = WID // NX
ZROW, ZCOL = RTOK // 2, XCOL // 4
EARLY = len(BATCHES[0]) * SLAB
PAIR = 2
XSUM = (1, 0, 0, 0, 0, 0, 1, 0)
XGATHER = (1, 1, 0, 0, 1, 0, 0, 1)
ORDER = (
    ("F", 0), ("F", 1), ("H",), ("E", 0), ("F", 2), ("E", 1), ("E", 2), ("C", 0), ("E", 3), ("F", 3), ("E", 4),
    ("X", 0, 0), ("X", 0, 1), ("C", 1), ("C", 2), ("C", 3), ("S", 0), ("E", 5), ("E", 6), ("S", 1), ("E", 7),
    ("S", 2), ("C", 4), ("T", 0), ("C", 5), ("C", 6), ("S", 3), ("T", 1), ("C", 7), ("K",), ("T", 2), ("S", 4),
    ("W", 0), ("A", 0), ("W", 1), ("S", 5), ("X", 6, 0), ("X", 6, 1), ("T", 3), ("W", 2), ("A", 1), ("A", 2),
    ("S", 7), ("L",), ("T", 4), ("B", 0, 0), ("B", 0, 1), ("S", 6), ("T", 5), ("W", 3), ("B", 1, 0),
    ("B", 1, 1), ("A", 3), ("O", 2), ("T", 7), ("O", 0), ("A", 4), ("O", 1), ("T", 6), ("A", 5), ("O", 3),
    ("B", 4, 0), ("B", 4, 1), ("A", 7), ("A", 6), ("O", 5), ("O", 4), ("B", 7, 0), ("B", 7, 1), ("O", 6),
    ("O", 7),
)


def dot(left, right, dims):
    return lax.dot_general(left, right, (dims, ((), ())), preferred_element_type=F32)


def kernel(
    x_hbm, g_hbm, wg_hbm, wu_hbm, wd_hbm, fin, gate_v, up_v, down_v,
    xv, gv, wgu, wd, xs, gs, yown, ysend, yrecv, ag, agsib, hall, hsib,
    xown, xacc, xsend, xone, xtwo, zsend, zrecv, load_sem, send_sem, recv_sem,
):
    dp, row, y = lax.axis_index("dp"), lax.axis_index("row"), lax.axis_index("col")
    z, x = row // NX, row % NX

    def at_y(k):
        return (dp, row, (y + k) % NY)

    def at_x(k):
        return (dp, z * NX + (x + k) % NX, y)

    def at_z(k):
        return (dp, ((z + k) % NZ) * NX + x, y)

    sibling = (1 - dp, row, y)

    barrier = pltpu.get_barrier_semaphore()
    partners = (
        [at_y(k) for k in range(1, NY)] + [at_x(k) for k in range(1, NX)] + [at_z(k) for k in range(1, NZ)] + [sibling]
    )
    for partner in partners:
        pl.semaphore_signal(barrier, inc=1, device_id=partner, device_id_type=MESH)

    loads = {}

    def load(name, src, dst):
        n = loads.setdefault(name, len(loads))
        pltpu.make_async_copy(src, dst, load_sem.at[n]).start()

    def loaded(name, ref):
        if name in loads:
            pltpu.make_async_copy(ref, ref, load_sem.at[loads.pop(name)]).wait()

    early, late = pl.ds(0, EARLY), pl.ds(EARLY, OWN - EARLY)
    rest = HID - CUT
    load("x0", x_hbm.at[:, early], xv.at[:, early])
    load("w", wg_hbm.at[pl.ds(0, CUT)], wgu.at[pl.ds(0, CUT)])
    load("w", wu_hbm.at[pl.ds(0, CUT)], wgu.at[pl.ds(CUT, CUT)])
    load("w", wg_hbm.at[pl.ds(CUT, rest)], wgu.at[pl.ds(2 * CUT, rest)])
    load("w", wu_hbm.at[pl.ds(CUT, rest)], wgu.at[pl.ds(CUT + HID, rest)])
    load("g0", g_hbm.at[:, early], gv.at[:, early])
    load("wd", wd_hbm, wd)
    load("x1", x_hbm.at[:, late], xv.at[:, late])
    load("g1", g_hbm.at[:, late], gv.at[:, late])

    sent, received = {}, {}

    def send(out, name, src, dst, device):
        n, m = sent.setdefault(out, len(sent)), received.setdefault(name, len(received))
        pltpu.make_async_remote_copy(
            src_ref=src, dst_ref=dst, send_sem=send_sem.at[n], recv_sem=recv_sem.at[m],
            device_id=device, device_id_type=MESH,
        ).start()

    def arrive(name, ref):
        pltpu.make_async_copy(ref, ref, recv_sem.at[received[name]]).wait()

    def slab(p):
        return pl.ds(p * SLAB, SLAB)

    def forward(i):
        first, n = BATCHES[i][0], len(BATCHES[i]) * SLAB
        part = pl.ds(first * SLAB, n)
        loaded("x0", xv.at[:, early])
        loaded("w", wgu)
        if i > 0:
            loaded("x1", xv.at[:, late])
        a = jnp.concatenate([xv[(y + k) % NY, part] for k in range(NY)], axis=0)
        both = dot(a, wgu[...], ((1,), (1,)))
        loaded("g0", gv.at[:, early])
        loaded("wd", wd)
        if i > 0:
            loaded("g1", gv.at[:, late])
        a = jnp.concatenate([gv[(y + k) % NY, part] for k in range(NY)], axis=0)
        hid = dot(a, wd[...], ((1,), (1,)))
        hid = jnp.concatenate((hid, jnp.zeros((NY * n, PACK - BOTH - HID), F32)), axis=1)
        for p in BATCHES[i]:
            start = (p - first) * SLAB
            for k in range(1, NY):
                mine = slice(k * n + start, k * n + start + SLAB)
                ysend[p, k - 1, :, :BOTH] = both[mine].astype(BF16)
                ysend[p, k - 1, :, BOTH:] = hid[mine].astype(BF16)
            if p == 0:
                pl.semaphore_wait(barrier, len(partners))
            for k in (2, 1, 3):
                send("yr", ("yr", p), ysend.at[p, k - 1], yrecv.at[p, k - 1], at_y(k))
            yown[p, :, :BOTH] = both[start : start + SLAB]
            yown[p, :, BOTH:] = hid[start : start + SLAB]

    def share():
        other = pl.ds(pl.multiple_of((1 - dp) * HALF, HALF), HALF)
        send("sx", "sx", xv.at[:, :, other], xs, sibling)
        send("sg", "sg", gv.at[:, :, other], gs, sibling)

    def swiglu_back(gate, up, hid):
        sig = jax.nn.sigmoid(gate)
        act = gate * sig
        return (
            (act * up).astype(BF16),
            (hid * up * sig * (1.0 + gate * (1.0 - sig))).astype(BF16),
            (hid * act).astype(BF16),
        )

    def elementwise(p):
        arrive(("yr", p), yrecv.at[p])
        total = yown[p] + yrecv[p, 0].astype(F32) + yrecv[p, 1].astype(F32) + yrecv[p, 2].astype(F32)
        hidden, gate, up = swiglu_back(
            total[:, :CUT], total[:, CUT : 2 * CUT], total[:, BOTH : BOTH + CUT]
        )
        ag[y, slab(p), :CUT] = gate
        ag[y, slab(p), CUT : 2 * CUT] = up
        hall[y, slab(p), :CUT] = hidden
        rest = HID - CUT
        hidden, gate, up = swiglu_back(
            total[:, 2 * CUT : 2 * CUT + rest], total[:, 2 * CUT + rest : BOTH], total[:, BOTH + CUT : BOTH + HID]
        )
        ag[y, slab(p), 2 * CUT :] = jnp.concatenate((gate, up), axis=1)
        hall[y, slab(p), CUT:] = jnp.concatenate((hidden, jnp.zeros_like(hidden)), axis=1)
        own = ag.at[y, slab(p)]
        for k in (2, 1, 3):
            send("yg", ("yg", p), own, own, at_y(k))

    def hidden_send():
        for k in (2, 1, 3):
            send("hg", "hg", hall.at[y], hall.at[y], at_y(k))

    def hidden_share():
        arrive("hg", hall.at[pl.ds(0, NY - 1)])
        send("hs", "hs", hall, hsib, sibling)

    def contract(p):
        arrive(("yg", p), ag.at[pl.ds(0, NY - 1), slab(p)])
        if p % PAIR == PAIR - 1:
            part = pl.ds((p - PAIR + 1) * SLAB, PAIR * SLAB)
            send("sd", "sd", ag.at[:, part], agsib.at[:, part], sibling)
        a = jnp.concatenate([ag[k, slab(p)] for k in range(NY)], axis=0)
        h = RTOK // 2
        lo, hi = pl.ds(0, h), pl.ds(h, h)
        for k in (2, 1, 3, 0):
            block = pl.ds(pl.multiple_of(((x + k) % NX) * XCOL, XCOL), XCOL)
            part = dot(a, wgu[:, block], ((1,), (0,)))
            if k == 0:
                xown[p] = part
                continue
            out = xsend.at[p, k - 1]
            out[...] = part.astype(BF16)
            if not XSUM[p]:
                send("xr", ("xr", p), out, xtwo.at[p, k - 1], at_x(k))
            elif k == 2:
                send("xr", ("x1", p, 0), out.at[lo], xone.at[p, 0], at_x(1))
                send("xr", ("x1", p, 1), out.at[hi], xone.at[p, 1], at_x(3))
            elif k == 1:
                xacc[p, 0] = part[:h]
                send("xr", ("xr", p), out.at[hi], xtwo.at[p, 0, hi], at_x(1))
            else:
                xacc[p, 1] = part[h:]
                send("xr", ("xr", p), out.at[lo], xtwo.at[p, 1, lo], at_x(3))

    def add_x(p, way):
        arrive(("x1", p, way), xone.at[p, way])
        h = RTOK // 2
        mine = pl.ds(way * h, h)
        out = xsend.at[p, 2 * way, mine]
        out[...] = (xacc[p, way] + xone[p, way].astype(F32)).astype(BF16)
        send("xr", ("xr", p), out, xtwo.at[p, way, mine], at_x(1 + 2 * way))

    def zplace(p, part):
        return (
            pl.ds(2 * (part // 4), 2),
            slab(p),
            pl.ds(pl.multiple_of(x * XCOL + (part % 4) * ZCOL, ZCOL), ZCOL),
        )

    def sum_x(p):
        if XSUM[p]:
            arrive(("xr", p), xtwo.at[p, pl.ds(0, 2)])
            total = xown[p] + xtwo[p, 0].astype(F32) + xtwo[p, 1].astype(F32)
        else:
            arrive(("xr", p), xtwo.at[p])
            total = xown[p] + xtwo[p, 0].astype(F32) + xtwo[p, 1].astype(F32) + xtwo[p, 2].astype(F32)
        xown[p] = total
        for k in (4, 3, 5, 2, 6, 1, 7):
            part = (z + k) % NZ
            zsend[p, k - 1] = xown[
                p,
                pl.ds(pl.multiple_of((part // 4) * ZROW, ZROW), ZROW),
                pl.ds(pl.multiple_of((part % 4) * ZCOL, ZCOL), ZCOL),
            ].astype(BF16)
            send("zr", ("zr", p), zsend.at[p, k - 1], zrecv.at[p, k - 1], at_z(k))

    def sum_z(p):
        arrive(("zr", p), zrecv.at[p])
        total = xown[
            p,
            pl.ds(pl.multiple_of((z // 4) * ZROW, ZROW), ZROW),
            pl.ds(pl.multiple_of((z % 4) * ZCOL, ZCOL), ZCOL),
        ]
        for k in range(1, NZ):
            total = total + zrecv[p, k - 1].astype(F32)
        place = zplace(p, z)
        fin[place] = total.astype(BF16).reshape(2, SLAB, ZCOL)
        for k in (4, 3, 5, 2, 6, 1, 7):
            send("za", ("za", p), fin.at[place], fin.at[place], at_z(k))

    def xplace(p, k, start, size):
        return fin.at[
            pl.ds(start, size), slab(p), pl.ds(pl.multiple_of(((x + k) % NX) * XCOL, XCOL), XCOL)
        ]

    def gather_x(p):
        arrive(("za", p), zrecv.at[p])
        place = xplace(p, 0, 0, NY)
        for k in (1, 3) if XGATHER[p] else (2, 1, 3):
            send("xg", ("xg", p, k) if XGATHER[p] else ("xg", p), place, place, at_x(k))

    def pass_x(p, way):
        arrive(("xg", p, 1 + 2 * way), xplace(p, 3 - 2 * way, 0, NY))
        place = xplace(p, 3 - 2 * way, 2 * way, 2)
        send("xg", ("xh", p), place, place, at_x(1 + 2 * way))

    def finish(p):
        if XGATHER[p]:
            arrive(("xh", p), xplace(p, 2, 0, NY))
        else:
            arrive(("xg", p), xtwo.at[p])

    def weights(i):
        if i == 0:
            arrive("sx", xs)
            arrive("sg", gs)
            arrive("sd", agsib)
        if i == 3:
            arrive("hs", hsib)
        half = pl.ds(pl.multiple_of(dp * HALF, HALF), HALF)
        start, size = ((0, CUT), (CUT, CUT), (2 * CUT, BOTH - 2 * CUT), (0, HID))[i]
        mine, theirs, own, sib = (hall, hsib, gv, gs) if i == 3 else (ag, agsib, xv, xs)
        cols = slice(start, start + size)
        total = dot(mine[:, :, cols].reshape(TOK, size), own[:, :, half].reshape(TOK, HALF), ((0,), (0,)))
        total += dot(theirs[:, :, cols].reshape(TOK, size), sib[...].reshape(TOK, HALF), ((0,), (0,)))
        total = total.astype(BF16)
        if i == 2:
            gate_v[CUT:, :] = total[:rest]
            up_v[CUT:, :] = total[rest:]
        else:
            (gate_v, up_v, None, down_v)[i][:size, :] = total

    tasks = {
        "F": forward, "H": share, "E": elementwise, "K": hidden_send, "L": hidden_share, "C": contract,
        "X": add_x, "S": sum_x, "T": sum_z, "A": gather_x, "B": pass_x, "O": finish, "W": weights,
    }
    for name, *args in ORDER:
        tasks[name](*args)
    for out, ref in (
        ("yr", ysend), ("yg", ag.at[pl.ds(0, NY - 1)]), ("hg", hall.at[pl.ds(0, NY - 1)]), ("xr", xsend),
        ("zr", zsend), ("za", zrecv), ("xg", xsend), ("sx", xs), ("sg", gs), ("sd", agsib), ("hs", hsib),
    ):
        pltpu.make_async_copy(ref, ref, send_sem.at[sent[out]]).wait()


def body(layer_input, out_grad, w_gate, w_up, w_down):
    n_received = 5 + 4 * ROUNDS + sum(3 if ring else 1 for ring in XSUM + XGATHER)
    in_grad, gate_grad, up_grad, down_grad = pl.pallas_call(
        kernel,
        out_shape=(
            pltpu.VMEM((NY, OWN, WID), BF16),
            pltpu.VMEM((HID, HALF), BF16),
            pltpu.VMEM((HID, HALF), BF16),
            pltpu.VMEM((HID, HALF), BF16),
        ),
        in_specs=[pl.BlockSpec(memory_space=pltpu.HBM)] * 5,
        out_specs=[pl.BlockSpec(memory_space=pltpu.VMEM)] * 4,
        scratch_shapes=[
            pltpu.VMEM((NY, OWN, WID), BF16),
            pltpu.VMEM((NY, OWN, WID), BF16),
            pltpu.VMEM((BOTH, WID), BF16),
            pltpu.VMEM((HID, WID), BF16),
            pltpu.VMEM((NY, OWN, HALF), BF16),
            pltpu.VMEM((NY, OWN, HALF), BF16),
            pltpu.VMEM((ROUNDS, SLAB, PACK), F32),
            pltpu.VMEM((ROUNDS, NY - 1, SLAB, PACK), BF16),
            pltpu.VMEM((ROUNDS, NY - 1, SLAB, PACK), BF16),
            pltpu.VMEM((NY, OWN, BOTH), BF16),
            pltpu.VMEM((NY, OWN, BOTH), BF16),
            pltpu.VMEM((NY, OWN, PACK - BOTH), BF16),
            pltpu.VMEM((NY, OWN, PACK - BOTH), BF16),
            pltpu.VMEM((ROUNDS, RTOK, XCOL), F32),
            pltpu.VMEM((ROUNDS, 2, RTOK // 2, XCOL), F32),
            pltpu.VMEM((ROUNDS, NX - 1, RTOK, XCOL), BF16),
            pltpu.VMEM((ROUNDS, 2, RTOK // 2, XCOL), BF16),
            pltpu.VMEM((ROUNDS, NX - 1, RTOK, XCOL), BF16),
            pltpu.VMEM((ROUNDS, NZ - 1, ZROW, ZCOL), BF16),
            pltpu.VMEM((ROUNDS, NZ - 1, ZROW, ZCOL), BF16),
            pltpu.SemaphoreType.DMA((6,)),
            pltpu.SemaphoreType.DMA((11,)),
            pltpu.SemaphoreType.DMA((n_received,)),
        ],
        compiler_params=pltpu.CompilerParams(
            collective_id=0, has_side_effects=True, vmem_limit_bytes=58 * 2**20
        ),
    )(
        layer_input.reshape(NY, OWN, WID), out_grad.reshape(NY, OWN, WID), w_gate.T, w_up.T, w_down,
    )
    return in_grad.reshape(TOK, WID), gate_grad.T, up_grad.T, down_grad


def solution(mesh):
    placed = (P("dp", "col"), P("dp", "col"), P("col", "row"), P("col", "row"), P("row", "col"))
    return jax.shard_map(
        body,
        mesh=mesh,
        in_specs=placed,
        out_specs=(
            P("dp", "col"),
            P(("col", "dp"), "row"),
            P(("col", "dp"), "row"),
            P("row", ("col", "dp")),
        ),
        check_vma=False,
    )
```

time: 303 us -> 72.6 us (0.24)
  blocking collectives: 210 us -> 0 us
  Pallas kernels: 0 us -> 67.2 us
  waiting for transfers between devices: 40.7 us -> 0 us
  matrix products: 21.9 us -> 0 us
  between operations: 13.8 us -> 0.64 us
  other arithmetic: 10.8 us -> 0 us
    psum x1 -> x0, blocking collectives: 172 us -> none  [body(): lax.psum(contract_cols(gate_all, w_gate) + contract_cols(up_all, w_up), '...]
    pallas_call x0 -> x1, Pallas kernels: none -> 67.2 us  [body(): pl.pallas_call(kernel, out_shape=(pltpu.VMEM((NY, OWN, WID), BF16), pltpu...]
    reduce_scatter x4 -> x0, waiting for transfers between devices: 40.7 us -> none  [the longest x1 40.7 us: body(): lax.psum_scatter(jnp.concatenate((gate_pre, up_pre, hid_grad), axis=1), '...]
    all_gather x3 -> x0, blocking collectives: 38.4 us -> none  [the longest x1 13 us: body(): lax.all_gather(hidden, 'col', axis=0, tiled=True)]
    dot_general x8 -> x0, matrix products: 21.9 us -> none  [the longest x3 10.6 us: contract_rows(): lax.dot_general(left, right, (((0,), (0,)), ((), ())), preferred_element_...]
    convert_element_type x4 -> x0, other arithmetic: 8.99 us -> none  [the longest x1 2.56 us: body(): gate_grad = gate_sum.astype(jnp.bfloat16)]
  transfers between devices with their start and end apart: 4 -> 0, of which waited for: 1 -> 0; matrix products, arithmetic and copies ran while one was open for 6% -> 0% of each run, Pallas kernels for 0% -> 0%
where the time goes in v3:
time: 72.6 us; the launch traced here: 71.9 us
  Pallas kernels  67.2 us (93%)
  local copies, waits for them, and re-layouts  4.09 us (6%)
    pallas_call x1, Pallas kernels, body(): pl.pallas_call(kernel, out_shape=(pltpu.VMEM((NY, OWN, WID), BF16), pltpu...  67.2 us
    unnamed x4, local copies, waits for them, and re-layouts  4.09 us

profile of v3, /device:TPU:2, one launch (start us, length us, event | category | flops | bytes accessed | tf_op | source)
XLA Modules:
  0.0 71.9 jit_solution(13138479803493520674)
XLA Ops:
  0.6 67.2 %shard_map.84 = (bf16[4,128,2048]{2,1,0:T(8,128)(2,1)S(1)}, bf16[448,1024]{1,0:T(8,128)(2,1)S(1)}, bf16[448,1024]{1,0:T(8,128)(2,1)S(1)}, bf16[448,1024]{1,0:T(8,128)(2,1)S(1)}) custom-call(bf16[4,128,2048]{2,1,0:T(8,128)(2,1)} %bitcast.10, bf16[4,128,2048]{2,1,0:T(8,128)(2,1)} %bitcast.11, bf16[448,2048]{1,0:T(8,128)(2,1)} %bitcast.12, ...), custom_call_target="tpu_custom_call" | custom-call | tf_op jit(solution)/shard_map/pallas_call | solution.py:307
  67.9 1.3 %copy.13 = bf16[512,2048]{1,0:T(8,128)(2,1)} copy(bf16[512,2048]{1,0:T(8,128)(2,1)S(1)} %bitcast.7) | data formatting | bytes 4194304
  69.2 0.9 %copy.14 = bf16[1024,448]{0,1:T(8,128)(2,1)} copy(bf16[1024,448]{0,1:T(8,128)(2,1)S(1)} %bitcast.9) | data formatting | bytes 1835008
  70.1 0.9 %copy.15 = bf16[1024,448]{0,1:T(8,128)(2,1)} copy(bf16[1024,448]{0,1:T(8,128)(2,1)S(1)} %bitcast.8) | data formatting | bytes 1835008
  71.0 0.9 %copy.16 = bf16[448,1024]{1,0:T(8,128)(2,1)} copy(bf16[448,1024]{1,0:T(8,128)(2,1)S(1)} %get-tuple-element.15) | data formatting | bytes 1835008

commit v4 on v3

--- a/solution.py
+++ b/solution.py
@@ -15,24 +15,24 @@
 HALF = WID // 2
 OWN = TOK // NY
 ROUNDS = 8
-BATCHES = ((0,), (1, 2), (3, 4), (5, 6, 7))
+BATCHES = ((0,), (1, 2), (3, 4), (5, 6), (7,))
 SLAB = OWN // ROUNDS
 RTOK = TOK // ROUNDS
 XCOL = WID // NX
 ZROW, ZCOL = RTOK // 2, XCOL // 4
 EARLY = len(BATCHES[0]) * SLAB
 PAIR = 2
-XSUM = (1, 0, 0, 0, 0, 0, 1, 0)
-XGATHER = (1, 1, 0, 0, 1, 0, 0, 1)
+XSUM = (1, 1, 0, 0, 0, 0, 0, 0)
+XGATHER = (1, 1, 1, 0, 1, 1, 1, 0)
 ORDER = (
-    ("F", 0), ("F", 1), ("H",), ("E", 0), ("F", 2), ("E", 1), ("E", 2), ("C", 0), ("E", 3), ("F", 3), ("E", 4),
-    ("X", 0, 0), ("X", 0, 1), ("C", 1), ("C", 2), ("C", 3), ("S", 0), ("E", 5), ("E", 6), ("S", 1), ("E", 7),
-    ("S", 2), ("C", 4), ("T", 0), ("C", 5), ("C", 6), ("S", 3), ("T", 1), ("C", 7), ("K",), ("T", 2), ("S", 4),
-    ("W", 0), ("A", 0), ("W", 1), ("S", 5), ("X", 6, 0), ("X", 6, 1), ("T", 3), ("W", 2), ("A", 1), ("A", 2),
-    ("S", 7), ("L",), ("T", 4), ("B", 0, 0), ("B", 0, 1), ("S", 6), ("T", 5), ("W", 3), ("B", 1, 0),
-    ("B", 1, 1), ("A", 3), ("O", 2), ("T", 7), ("O", 0), ("A", 4), ("O", 1), ("T", 6), ("A", 5), ("O", 3),
-    ("B", 4, 0), ("B", 4, 1), ("A", 7), ("A", 6), ("O", 5), ("O", 4), ("B", 7, 0), ("B", 7, 1), ("O", 6),
-    ("O", 7),
+    ("F", 0), ("F", 1), ("H",), ("E", 0), ("E", 1), ("F", 2), ("E", 2), ("C", 0), ("C", 1), ("E", 3), ("F", 3),
+    ("X", 0, 0), ("X", 0, 1), ("E", 4), ("X", 1, 0), ("X", 1, 1), ("C", 2), ("C", 3), ("S", 0), ("S", 1),
+    ("E", 5), ("F", 4), ("E", 6), ("S", 2), ("C", 4), ("C", 5), ("T", 0), ("S", 3), ("T", 1), ("E", 7),
+    ("C", 6), ("T", 2), ("S", 4), ("C", 7), ("K",), ("A", 0), ("S", 5), ("T", 3), ("W", 0), ("W", 1), ("S", 6),
+    ("W", 2), ("A", 1), ("A", 2), ("T", 4), ("S", 7), ("T", 5), ("B", 0, 0), ("B", 0, 1), ("A", 3), ("L",),
+    ("B", 1, 0), ("B", 1, 1), ("T", 6), ("W", 3), ("O", 0), ("B", 2, 0), ("B", 2, 1), ("A", 4), ("T", 7),
+    ("A", 5), ("O", 3), ("O", 1), ("A", 6), ("O", 2), ("B", 4, 0), ("B", 4, 1), ("A", 7), ("B", 5, 0),
+    ("B", 5, 1), ("B", 6, 0), ("B", 6, 1), ("O", 4), ("O", 7), ("O", 5), ("O", 6),
 )
 
 
@@ -300,6 +300,15 @@
         ("zr", zsend), ("za", zrecv), ("xg", xsend), ("sx", xs), ("sg", gs), ("sd", agsib), ("hs", hsib),
     ):
         pltpu.make_async_copy(ref, ref, send_sem.at[sent[out]]).wait()
+
+
+def write_out(*refs):
+    sems = refs[8]
+    copies = [pltpu.make_async_copy(refs[i], refs[4 + i], sems.at[i]) for i in range(4)]
+    for copy in copies:
+        copy.start()
+    for copy in copies:
+        copy.wait()
 
 
 def body(layer_input, out_grad, w_gate, w_up, w_down):
@@ -345,6 +354,14 @@
     )(
         layer_input.reshape(NY, OWN, WID), out_grad.reshape(NY, OWN, WID), w_gate.T, w_up.T, w_down,
     )
+    in_grad, gate_grad, up_grad, down_grad = pl.pallas_call(
+        write_out,
+        out_shape=[jax.ShapeDtypeStruct(a.shape, a.dtype) for a in (in_grad, gate_grad, up_grad, down_grad)],
+        in_specs=[pl.BlockSpec(memory_space=pltpu.VMEM)] * 4,
+        out_specs=[pl.BlockSpec(memory_space=pl.ANY)] * 4,
+        scratch_shapes=[pltpu.SemaphoreType.DMA((4,))],
+        compiler_params=pltpu.CompilerParams(vmem_limit_bytes=2**20),
+    )(in_grad, gate_grad, up_grad, down_grad)
     return in_grad.reshape(TOK, WID), gate_grad.T, up_grad.T, down_grad
 
 

time: 72.6 us -> 69.4 us (0.956)
  local copies, waits for them, and re-layouts: 4.09 us -> 0 us
    unnamed x4 -> x0, local copies, waits for them, and re-layouts: 4.09 us -> none
    pallas_call x0 -> x1, Pallas kernels: none -> 2.25 us  [body(): pl.pallas_call(write_out, out_shape=[jax.ShapeDtypeStruct(a.shape, a.dtyp...]
    pallas_call x1, Pallas kernels: 67.2 us -> 65.3 us  [body(): pl.pallas_call(kernel, out_shape=(pltpu.VMEM((NY, OWN, WID), BF16), pltpu...]
where the time goes in v4:
time: 69.4 us; the launch traced here: 68.4 us
  Pallas kernels  67.6 us (97%)
  between operations  0.8 us (1%)
    pallas_call x1, Pallas kernels, body(): pl.pallas_call(kernel, out_shape=(pltpu.VMEM((NY, OWN, WID), BF16), pltpu...  65.3 us
    pallas_call x1, Pallas kernels, body(): pl.pallas_call(write_out, out_shape=[jax.ShapeDtypeStruct(a.shape, a.dtyp...  2.25 us

profile of v4, /device:TPU:2, one launch (start us, length us, event | category | flops | bytes accessed | tf_op | source)
XLA Modules:
  0.0 68.4 jit_solution(7790356144881121808)
XLA Ops:
  0.6 65.3 %shard_map.84 = (bf16[4,128,2048]{2,1,0:T(8,128)(2,1)S(1)}, bf16[448,1024]{1,0:T(8,128)(2,1)S(1)}, bf16[448,1024]{1,0:T(8,128)(2,1)S(1)}, bf16[448,1024]{1,0:T(8,128)(2,1)S(1)}) custom-call(bf16[4,128,2048]{2,1,0:T(8,128)(2,1)} %bitcast.7, bf16[4,128,2048]{2,1,0:T(8,128)(2,1)} %bitcast.8, bf16[448,2048]{1,0:T(8,128)(2,1)} %bitcast.9, ...), custom_call_target="tpu_custom_call" | custom-call | tf_op jit(solution)/shard_map/pallas_call | solution.py:316
  66.0 2.3 %shard_map.85 = (bf16[4,128,2048]{2,1,0:T(8,128)(2,1)}, bf16[448,1024]{1,0:T(8,128)(2,1)}, bf16[448,1024]{1,0:T(8,128)(2,1)}, bf16[448,1024]{1,0:T(8,128)(2,1)}) custom-call(bf16[4,128,2048]{2,1,0:T(8,128)(2,1)S(1)} %get-tuple-element.12.refs_0_, bf16[448,1024]{1,0:T(8,128)(2,1)S(1)} %get-tuple-element.13.refs_1_, ...), custom_call_target="tpu_custom_call" | custom-call | tf_op jit(solution)/shard_map/pallas_call | solution.py:357

commit v5 on v4

--- a/solution.py
+++ b/solution.py
@@ -28,11 +28,11 @@
     ("F", 0), ("F", 1), ("H",), ("E", 0), ("E", 1), ("F", 2), ("E", 2), ("C", 0), ("C", 1), ("E", 3), ("F", 3),
     ("X", 0, 0), ("X", 0, 1), ("E", 4), ("X", 1, 0), ("X", 1, 1), ("C", 2), ("C", 3), ("S", 0), ("S", 1),
     ("E", 5), ("F", 4), ("E", 6), ("S", 2), ("C", 4), ("C", 5), ("T", 0), ("S", 3), ("T", 1), ("E", 7),
-    ("C", 6), ("T", 2), ("S", 4), ("C", 7), ("K",), ("A", 0), ("S", 5), ("T", 3), ("W", 0), ("W", 1), ("S", 6),
-    ("W", 2), ("A", 1), ("A", 2), ("T", 4), ("S", 7), ("T", 5), ("B", 0, 0), ("B", 0, 1), ("A", 3), ("L",),
-    ("B", 1, 0), ("B", 1, 1), ("T", 6), ("W", 3), ("O", 0), ("B", 2, 0), ("B", 2, 1), ("A", 4), ("T", 7),
-    ("A", 5), ("O", 3), ("O", 1), ("A", 6), ("O", 2), ("B", 4, 0), ("B", 4, 1), ("A", 7), ("B", 5, 0),
-    ("B", 5, 1), ("B", 6, 0), ("B", 6, 1), ("O", 4), ("O", 7), ("O", 5), ("O", 6),
+    ("C", 6), ("T", 2), ("S", 4), ("C", 7), ("K",), ("S", 5), ("T", 3), ("S", 6), ("A", 0), ("A", 1), ("A", 2),
+    ("T", 4), ("S", 7), ("T", 5), ("B", 0, 0), ("B", 0, 1), ("A", 3), ("B", 1, 0), ("B", 1, 1), ("T", 6),
+    ("B", 2, 0), ("B", 2, 1), ("A", 4), ("T", 7), ("W", 0), ("A", 5), ("W", 1), ("L",), ("A", 6), ("W", 2),
+    ("B", 4, 0), ("B", 4, 1), ("A", 7), ("W", 3), ("B", 5, 0), ("B", 5, 1), ("B", 6, 0), ("B", 6, 1), ("O", 0),
+    ("O", 1), ("O", 2), ("O", 3), ("O", 4), ("O", 5), ("O", 6), ("O", 7),
 )
 
 

time: 69.4 us -> 69.4 us (level)
  the two profiles are of different devices: /device:TPU:2 before, /device:TPU:1 now
where the time goes in v5:
time: 69.4 us; the launch traced here: 69.3 us
  Pallas kernels  68.5 us (99%)
  between operations  0.8 us (1%)
    pallas_call x1, Pallas kernels, body(): pl.pallas_call(kernel, out_shape=(pltpu.VMEM((NY, OWN, WID), BF16), pltpu...  66.2 us
    pallas_call x1, Pallas kernels, body(): pl.pallas_call(write_out, out_shape=[jax.ShapeDtypeStruct(a.shape, a.dtyp...  2.25 us

profile of v5, /device:TPU:1, one launch (start us, length us, event | category | flops | bytes accessed | tf_op | source)
XLA Modules:
  0.0 69.3 jit_solution(8101119848903608051)
XLA Ops:
  0.6 66.2 %shard_map.84 = (bf16[4,128,2048]{2,1,0:T(8,128)(2,1)S(1)}, bf16[448,1024]{1,0:T(8,128)(2,1)S(1)}, bf16[448,1024]{1,0:T(8,128)(2,1)S(1)}, bf16[448,1024]{1,0:T(8,128)(2,1)S(1)}) custom-call(bf16[4,128,2048]{2,1,0:T(8,128)(2,1)} %bitcast.7, bf16[4,128,2048]{2,1,0:T(8,128)(2,1)} %bitcast.8, bf16[448,2048]{1,0:T(8,128)(2,1)} %bitcast.9, ...), custom_call_target="tpu_custom_call" | custom-call | tf_op jit(solution)/shard_map/pallas_call | solution.py:316
  66.9 2.3 %shard_map.85 = (bf16[4,128,2048]{2,1,0:T(8,128)(2,1)}, bf16[448,1024]{1,0:T(8,128)(2,1)}, bf16[448,1024]{1,0:T(8,128)(2,1)}, bf16[448,1024]{1,0:T(8,128)(2,1)}) custom-call(bf16[4,128,2048]{2,1,0:T(8,128)(2,1)S(1)} %get-tuple-element.12.refs_0_, bf16[448,1024]{1,0:T(8,128)(2,1)S(1)} %get-tuple-element.13.refs_1_, ...), custom_call_target="tpu_custom_call" | custom-call | tf_op jit(solution)/shard_map/pallas_call | solution.py:357
